TPU v7x, 32 devices: a whole 2x2x4 slice. The times are simulated.
32 devices in a mesh: lon: 16 (over z, x, core), lat: 2 (over y).
Axes of the slice: x: 2, y: 2, z: 4, core: 2. Of those that a mesh axis runs over, the one named last changes fastest.
Arguments:
- potential_heat: float32 [8, 256, 2048], P(None, 'lat', 'lon'), may hold values from -6 to 6
- saltiness_anomaly: float32 [8, 256, 2048], P(None, 'lat', 'lon'), may hold values from -6 to 6
- east_current: float32 [8, 256, 2048], P(None, 'lat', 'lon'), may hold values from -1 to 1
- north_current: float32 [8, 256, 2048], P(None, 'lat', 'lon'), may hold values from -1 to 1
- water_indicator: int32 [8, 256, 2048], P(None, 'lat', 'lon'), may hold values from 0 to 1, as said below
- east_west_courant_factor: float32 [256, 2048], P('lat', 'lon'), may hold values from 0.05 to 0.45
- north_south_courant_factor: float32 [256, 2048], P('lat', 'lon'), may hold values from 0.05 to 0.45
- interface_diffusion_factor: float32 [7, 256, 2048], P(None, 'lat', 'lon'), may hold values from 0.05 to 5
- spreading_coefficient: float32 [4, 8], replicated, may hold values from 0.05 to 0.25
- seam_mirror_index: int32 [2048], P('lon'), may hold values from 0 to 2047, as said below
Outputs:
- temperature_next: float32 [8, 256, 2048], P(None, 'lat', 'lon')
- salinity_next: float32 [8, 256, 2048], P(None, 'lat', 'lon')
- zonal_next: float32 [8, 256, 2048], P(None, 'lat', 'lon')
- meridional_next: float32 [8, 256, 2048], P(None, 'lat', 'lon')
Inputs may be any that keep to these rules, and one draw needn't show every extreme that they name: water_indicator is 0 or 1, and a cell below a land cell is land. seam_mirror_index[i] = (p - i) mod 2048 for one p whose remainder on division by 128 is 127.
All inputs are finite; a program needn't handle non-finite values.
Results may differ from a plain program's by a relative error of at most 0.0003.
Values sent between devices are 32-bit elements; how exact they have to be, the bound alone decides.
A program may use at most 128 MiB of HBM per device.

v0:
```python
import jax
import jax.numpy as jnp
from jax import lax
from jax.sharding import PartitionSpec as P


def extended_2(cells, sides, width, closed):
    for axis, dim in sides:
        count = lax.axis_size(axis)
        ends = count if closed else count - 1
        head = lax.slice_in_dim(cells, 0, width, axis=dim)
        tail = lax.slice_in_dim(cells, cells.shape[dim] - width, cells.shape[dim], axis=dim)
        cells = jnp.concatenate(
            [
                lax.ppermute(tail, axis, [(i, (i + 1) % count) for i in range(ends)]),
                cells,
                lax.ppermute(head, axis, [((i + 1) % count, i) for i in range(ends)]),
            ],
            axis=dim,
        )
    return cells


def cut(source, first_index, last_index, dimension):
    return lax.slice_in_dim(source, first_index, last_index, axis=dimension)


def ppm_update(extended, courant, opening, dimension):
    length = extended.shape[dimension] - 6
    edge_value = 7.0 / 12.0 * (
        cut(extended, 1, length + 4, dimension) + cut(extended, 2, length + 5, dimension)
    ) - 1.0 / 12.0 * (
        cut(extended, 0, length + 3, dimension) + cut(extended, 3, length + 6, dimension)
    )
    left_edge = cut(edge_value, 0, length + 2, dimension)
    right_edge = cut(edge_value, 1, length + 3, dimension)
    centre = cut(extended, 2, length + 4, dimension)
    slopes = right_edge - left_edge
    curvature = 6.0 * (centre - 0.5 * (left_edge + right_edge))
    courant_size = jnp.abs(courant)
    shape_factor = 1.0 - 2.0 / 3.0 * courant_size
    from_left = cut(right_edge, 0, length + 1, dimension) - 0.5 * courant_size * (
        cut(slopes, 0, length + 1, dimension)
        - shape_factor * cut(curvature, 0, length + 1, dimension)
    )
    from_right = cut(left_edge, 1, length + 2, dimension) + 0.5 * courant_size * (
        cut(slopes, 1, length + 2, dimension)
        + shape_factor * cut(curvature, 1, length + 2, dimension)
    )
    fluxes = courant * opening * jnp.where(courant >= 0.0, from_left, from_right)
    return cut(fluxes, 0, length, dimension) - cut(fluxes, 1, length + 1, dimension)


def face_terms(speed_metric, wet_ext, metric_ext, dimension):
    length = wet_ext.shape[dimension] - 6
    courant = 0.5 * (
        cut(speed_metric, 2, length + 3, dimension) + cut(speed_metric, 3, length + 4, dimension)
    )
    opening = cut(wet_ext, 2, length + 3, dimension) * cut(wet_ext, 3, length + 4, dimension)
    weight = (
        0.5
        * (cut(metric_ext, 2, length + 3, dimension) + cut(metric_ext, 3, length + 4, dimension))
        * opening
    )
    return (courant, opening, weight)


def vertical_solve(target_rhs, coupling):
    layer_total = target_rhs.shape[1]
    zeros_plane = jnp.zeros_like(target_rhs[:, 0])
    factors = []
    reduced = []
    for layer_index in range(layer_total):
        upward = coupling[layer_index - 1] if layer_index > 0 else zeros_plane
        downward = coupling[layer_index] if layer_index < layer_total - 1 else zeros_plane
        divisor = 1.0 + upward + downward
        target = target_rhs[:, layer_index]
        if layer_index > 0:
            divisor = divisor - upward * factors[layer_index - 1]
            target = target + upward * reduced[layer_index - 1]
        factors.append(downward / divisor)
        reduced.append(target / divisor)
    solved_levels = [reduced[layer_total - 1]]
    for layer_index in range(layer_total - 2, -1, -1):
        solved_levels.insert(0, reduced[layer_index] + factors[layer_index] * solved_levels[0])
    return jnp.stack(solved_levels, axis=1)


def fold_rows(block_rows, seam_mirror_index, meridian_total):
    whole_rows = lax.all_gather(block_rows, "lon", axis=2, tiled=True)
    span = block_rows.shape[2]
    tile_number = seam_mirror_index[0] // meridian_total
    piece = lax.dynamic_slice_in_dim(whole_rows, tile_number * span, span, 2)
    return piece[:, :, ::-1]


def shards(
    potential_heat,
    saltiness_anomaly,
    east_current,
    north_current,
    water_indicator,
    east_west_courant_factor,
    north_south_courant_factor,
    interface_diffusion_factor,
    spreading_coefficient,
    seam_mirror_index,
):
    layer_total, parallel_total, meridian_total = potential_heat.shape
    margin = 0
    reach = 3 + margin
    span = meridian_total + 2 * margin
    rise = parallel_total + 2 * margin
    ocean_point_indicator = water_indicator.astype(jnp.float32)
    transported_quantities = jnp.concatenate(
        [
            potential_heat * ocean_point_indicator,
            saltiness_anomaly * ocean_point_indicator,
            east_current * ocean_point_indicator,
            north_current * ocean_point_indicator,
        ],
        axis=0,
    )
    first_stack = jnp.concatenate(
        [
            transported_quantities,
            ocean_point_indicator,
            east_west_courant_factor[None],
            north_south_courant_factor[None],
        ],
        axis=0,
    )
    wide_stack = extended_2(first_stack, (("lon", 2),), reach, True)
    field_x = wide_stack[: 4 * layer_total].reshape(
        4, layer_total, parallel_total, meridian_total + 2 * reach
    )
    wet_x = wide_stack[4 * layer_total : 5 * layer_total]
    metric_x = wide_stack[5 * layer_total : 5 * layer_total + 1]
    speed_x = field_x[2] * metric_x
    courant_x, opening_x, weight_x = face_terms(speed_x, wet_x, metric_x, 2)
    starred = cut(field_x, 3, 3 + span, 3) + ppm_update(field_x, courant_x, opening_x, 3)
    side_planes = cut(wide_stack[3 * layer_total : 5 * layer_total], 3, 3 + span, 2)
    merid_planes = cut(wide_stack[5 * layer_total + 1 :], 3, 3 + span, 2)
    second = jnp.concatenate(
        [starred.reshape(4 * layer_total, parallel_total, span), side_planes, merid_planes], axis=0
    )
    signs_two = jnp.concatenate(
        [
            jnp.ones((2 * layer_total, 1, 1), jnp.float32),
            -jnp.ones((3 * layer_total, 1, 1), jnp.float32),
            jnp.ones((layer_total + 1, 1, 1), jnp.float32),
        ],
        axis=0,
    )
    tall_stack = extended_2(second, (("lat", 1),), reach, False)
    upper_rows = (
        fold_rows(
            second[:, parallel_total - reach :, :][:, ::-1, :], seam_mirror_index, meridian_total
        )
        * signs_two
    )
    northern = lax.axis_index("lat") == lax.axis_size("lat") - 1
    southern = lax.axis_index("lat") == 0
    tall_stack = jnp.concatenate(
        [
            tall_stack[:, : parallel_total + reach],
            jnp.where(northern, upper_rows, tall_stack[:, parallel_total + reach :]),
        ],
        axis=1,
    )
    field_y = tall_stack[: 4 * layer_total].reshape(
        4, layer_total, parallel_total + 2 * reach, span
    )
    merid_speed = tall_stack[4 * layer_total : 5 * layer_total]
    wet_y = tall_stack[5 * layer_total : 6 * layer_total]
    metric_y = tall_stack[6 * layer_total :]
    courant_y, opening_y, weight_y = face_terms(merid_speed * metric_y, wet_y, metric_y, 1)
    advected = cut(field_y, 3, 3 + rise, 2) + ppm_update(field_y, courant_y, opening_y, 2)
    flat_fields = advected.reshape(4 * layer_total, parallel_total, meridian_total)
    near_stack = extended_2(flat_fields, (("lon", 2), ("lat", 1)), 1, True)
    signs_one = signs_two[: 4 * layer_total]
    upper_row = (
        fold_rows(flat_fields[:, parallel_total - 1 :, :], seam_mirror_index, meridian_total)
        * signs_one
    )
    rows_flat = near_stack[:, :, 1:-1]
    lower_row = jnp.where(southern, jnp.zeros_like(rows_flat[:, :1]), rows_flat[:, :1])
    upper_row = jnp.where(northern, upper_row, rows_flat[:, parallel_total + 1 :])
    rows_ext = jnp.concatenate(
        [lower_row, rows_flat[:, 1 : parallel_total + 1], upper_row], axis=1
    ).reshape(4, layer_total, parallel_total + 2, meridian_total)
    cols_ext = near_stack[:, 1:-1, :].reshape(4, layer_total, parallel_total, meridian_total + 2)
    laplacian = (
        weight_x[:, :, 1:] * (cols_ext[..., 2:] - advected)
        - weight_x[:, :, :-1] * (advected - cols_ext[..., :-2])
        + weight_y[:, 1:, :] * (rows_ext[:, :, 2:, :] - advected)
        - weight_y[:, :-1, :] * (advected - rows_ext[:, :, :-2, :])
    )
    diffused = advected + spreading_coefficient[:, :, None, None] * laplacian
    coupling = interface_diffusion_factor * ocean_point_indicator[:-1] * ocean_point_indicator[1:]
    solved = vertical_solve(diffused, coupling) * ocean_point_indicator
    return (solved[0], solved[1], solved[2], solved[3])


def solution(mesh):
    in_specs = (
        P(None, "lat", "lon"),
        P(None, "lat", "lon"),
        P(None, "lat", "lon"),
        P(None, "lat", "lon"),
        P(None, "lat", "lon"),
        P("lat", "lon"),
        P("lat", "lon"),
        P(None, "lat", "lon"),
        P(),
        P("lon"),
    )
    out_specs = (
        P(None, "lat", "lon"),
        P(None, "lat", "lon"),
        P(None, "lat", "lon"),
        P(None, "lat", "lon"),
    )
    return jax.shard_map(shards, mesh=mesh, in_specs=in_specs, out_specs=out_specs, check_vma=False)
```

profile of v0, /device:TPU:1, one launch (start us, length us, event | category | flops | bytes accessed | tf_op | source)
XLA Modules:
  0.0 154.1 jit_solution(8113493135407625695)
XLA Ops:
  7.2 1.3 copy.85
  8.6 2.0 %copy.86 = f32[8,128,128]{1,2,0:T(8,128)} copy(f32[8,128,128]{2,1,0:T(8,128)} %param.10) | data formatting | bytes 1048576 | tf_op args[0]
  17.3 2.7 %collective-permute-start = (f32[42,128,3]{1,0,2:T(8,128)S(1)}, f32[42,128,3]{1,0,2:T(8,128)S(1)}, u32[]{:S(2)}, u32[]{:S(2)}) collective-permute-start(f32[42,128,3]{1,0,2:T(8,128)S(1)} %copy.92), channel_id=1, source_target_pairs={{0,2},{2,4},{4,6},{6,8},{8,10},{10,12},{12,14},{14,16},{16,18},{18... | collective-permute-start | bytes 193544 | tf_op jit(solution)/shard_map/ppermute | solution.py:15
  21.4 2.0 %copy.99 = f32[8,128,128]{2,1,0:T(8,128)} copy(f32[8,128,128]{1,2,0:T(8,128)} %get-tuple-element.33) | data formatting | bytes 1048576 | tf_op jit(solution)/shard_map/mul | solution.py:120
  23.4 1.2 copy.100
  29.3 1.3 fusion.16
  30.6 1.8 %fusion.38 = f32[4,8,128,128]{2,3,1,0:T(8,128)} fusion(f32[4,8,128,129]{2,3,1,0:T(8,128)S(1)} %fusion.16, f32[4,8,128,134]{2,3,1,0:T(8,128)S(1)} %bitcast.115), kind=kLoop, calls=%fused_computation.57 | loop fusion | flops 1048576 | bytes 8388608 | tf_op jit(solution)/shard_map/add | solution.py:141
  32.5 2.0 %copy.98 = f32[32,128,128]{2,1,0:T(8,128)S(1)} copy(f32[32,128,128]{1,2,0:T(8,128)} %bitcast.119) | data formatting | bytes 4194304 | tf_op jit(solution)/shard_map/reshape | solution.py:145
  36.1 2.0 %copy.112 = f32[7,128,128]{1,2,0:T(8,128)} copy(f32[7,128,128]{2,1,0:T(8,128)} %param.17) | data formatting | bytes 917504 | tf_op args[7]
  38.1 1.4 slice_multiply_fusion.4
  43.7 1.6 %copy.132 = f32[128,128]{1,0:T(8,128)} copy(f32[128,128]{0,1:T(8,128)} %get-tuple-element.12) | data formatting | bytes 131072 | tf_op jit(solution)/shard_map/div | solution.py:81
  45.3 1.6 %copy.113 = f32[128,128]{1,0:T(8,128)} copy(f32[128,128]{0,1:T(8,128)} %get-tuple-element.68) | data formatting | bytes 131072 | tf_op jit(solution)/shard_map/add;add | solution.py:76
  46.8 1.6 %copy.114 = f32[128,128]{1,0:T(8,128)} copy(f32[128,128]{0,1:T(8,128)} %get-tuple-element.67) | data formatting | bytes 131072 | tf_op jit(solution)/shard_map/div | solution.py:81
  48.4 1.6 %copy.116 = f32[128,128]{1,0:T(8,128)} copy(f32[128,128]{0,1:T(8,128)} %get-tuple-element.23) | data formatting | bytes 131072 | tf_op jit(solution)/shard_map/sub | solution.py:79
  50.0 1.6 %copy.117 = f32[128,128]{1,0:T(8,128)} copy(f32[128,128]{0,1:T(8,128)} %get-tuple-element.22) | data formatting | bytes 131072 | tf_op jit(solution)/shard_map/div | solution.py:81
  51.5 1.6 %copy.119 = f32[128,128]{1,0:T(8,128)} copy(f32[128,128]{0,1:T(8,128)} %get-tuple-element.21) | data formatting | bytes 131072 | tf_op jit(solution)/shard_map/sub | solution.py:79
  53.1 1.6 %copy.122 = f32[128,128]{1,0:T(8,128)} copy(f32[128,128]{0,1:T(8,128)} %get-tuple-element.19) | data formatting | bytes 131072 | tf_op jit(solution)/shard_map/sub | solution.py:79
  54.6 1.6 %copy.123 = f32[128,128]{1,0:T(8,128)} copy(f32[128,128]{0,1:T(8,128)} %get-tuple-element.18) | data formatting | bytes 131072 | tf_op jit(solution)/shard_map/div | solution.py:81
  56.2 1.6 %copy.125 = f32[128,128]{1,0:T(8,128)} copy(f32[128,128]{0,1:T(8,128)} %get-tuple-element.17) | data formatting | bytes 131072 | tf_op jit(solution)/shard_map/sub | solution.py:79
  57.7 1.6 %copy.128 = f32[128,128]{1,0:T(8,128)} copy(f32[128,128]{0,1:T(8,128)} %get-tuple-element.15) | data formatting | bytes 131072 | tf_op jit(solution)/shard_map/sub | solution.py:79
  59.3 1.6 %copy.129 = f32[128,128]{1,0:T(8,128)} copy(f32[128,128]{0,1:T(8,128)} %get-tuple-element.14) | data formatting | bytes 131072 | tf_op jit(solution)/shard_map/div | solution.py:81
  61.6 1.8 %slice_bitcast_fusion.10 = (f32[128,128]{0,1:T(8,128)}, f32[128,128]{0,1:T(8,128)}, f32[128,128]{0,1:T(8,128)S(1)}, f32[128,128]{0,1:T(8,128)}, f32[128,128]{0,1...) fusion(f32[7,128,128]{1,2,0:T(8,128)} %copy-done.3), kind=kLoop, calls=%fused_computation.148 | loop fusion | bytes 917504 | tf_op jit(solution)/shard_map/div | solution.py:81
  64.2 1.6 %copy.115 = f32[128,128]{1,0:T(8,128)} copy(f32[128,128]{0,1:T(8,128)} %get-tuple-element.66) | data formatting | bytes 131072 | tf_op jit(solution)/shard_map/add | solution.py:76
  65.8 1.6 %copy.118 = f32[128,128]{1,0:T(8,128)} copy(f32[128,128]{0,1:T(8,128)} %get-tuple-element.60) | data formatting | bytes 131072 | tf_op jit(solution)/shard_map/div | solution.py:81
  67.4 1.6 %copy.121 = f32[128,128]{1,0:T(8,128)} copy(f32[128,128]{0,1:T(8,128)} %get-tuple-element.63) | data formatting | bytes 131072 | tf_op jit(solution)/shard_map/div | solution.py:81
  68.9 1.6 %copy.124 = f32[128,128]{1,0:T(8,128)} copy(f32[128,128]{0,1:T(8,128)} %get-tuple-element.65) | data formatting | bytes 131072 | tf_op jit(solution)/shard_map/div | solution.py:81
  71.9 3.6 %collective-permute-start.2 = (f32[49,3,128]{2,1,0:T(4,128)}, f32[49,3,128]{2,1,0:T(4,128)S(1)}, u32[]{:S(2)}, u32[]{:S(2)}) collective-permute-start(f32[49,3,128]{2,1,0:T(4,128)} %copy-done.12), channel_id=1, source_target_pairs={{0,1},{2,3},{4,5},{6,7},{8,9},{10,11},{12,13},{14,15},{16,17},{18,... | collective-permute-start | bytes 225800 | tf_op jit(solution)/shard_map/ppermute | solution.py:15
  75.5 1.5 collective-permute-start.3
  77.0 2.3 %fusion.78 = (f32[8,128,128]{1,2,0:T(8,128)}, f32[8,128,128]{1,2,0:T(8,128)}) fusion(f32[8,128,129]{1,2,0:T(8,128)} %get-tuple-element.24), kind=kLoop, calls=%fused_computation.172 | loop fusion | bytes 2097152 | tf_op jit(solution)/shard_map/slice | solution.py:194
  79.3 2.0 %copy.102 = f32[8,128,128]{2,1,0:T(8,128)} copy(f32[8,128,128]{1,2,0:T(8,128)} %get-tuple-element.50) | data formatting | bytes 1048576 | tf_op jit(solution)/shard_map/slice | solution.py:194
  81.3 2.0 %copy.105 = f32[8,128,128]{2,1,0:T(8,128)} copy(f32[8,128,128]{1,2,0:T(8,128)} %get-tuple-element.51) | data formatting | bytes 1048576 | tf_op jit(solution)/shard_map/slice | solution.py:195
  83.4 1.6 %constant_dynamic-slice_fusion.1 = f32[49,3,128]{2,1,0:T(4,128)} fusion(f32[49,3,2048]{2,1,0:T(4,128)} %all-gather.2.cloned.1.call-done, s32[]{:T(128)S(6)} %select_n.43), kind=kLoop, calls=%fused_computation.161 | loop fusion | bytes 150532 | tf_op jit(solution)/shard_map/dynamic_slice | solution.py:93
  84.9 1.7 %rev.10 = f32[49,3,128]{2,1,0:T(4,128)} reverse(f32[49,3,128]{2,1,0:T(4,128)} %constant_dynamic-slice_fusion.1), dimensions={2} | reverse | bytes 150528 | tf_op jit(solution)/shard_map/rev | solution.py:94
  91.2 1.2 fusion.4
  92.4 1.9 %fusion.37 = f32[4,8,128,128]{3,2,1,0:T(8,128)} fusion(f32[4,8,129,128]{3,2,1,0:T(8,128)S(1)} %fusion.4, f32[4,8,134,128]{3,2,1,0:T(8,128)S(1)} %bitcast.112), kind=kLoop, calls=%fused_computation.55 | loop fusion | flops 1048576 | bytes 8388608 | tf_op jit(solution)/shard_map/add | solution.py:178
  94.2 2.4 %copy.103 = f32[4,8,128,128]{2,1,0,3:T(8,128)S(1)} copy(f32[4,8,128,128]{3,2,1,0:T(8,128)} %fusion.37) | data formatting | bytes 4194304 | tf_op jit(solution)/shard_map/add | solution.py:178
  96.6 2.0 %slice.455 = f32[32,1,128]{1,0,2:T(8,128)} slice(f32[32,128,128]{1,0,2:T(8,128)S(1)} %bitcast.117), slice={[0:32], [127:128], [0:128]} | slice | bytes 32768 | tf_op jit(solution)/shard_map/slice | solution.py:183
  98.6 3.0 %collective-permute-start.4 = (f32[32,128,1]{1,0,2:T(8,128)S(1)}, f32[32,128,1]{1,0,2:T(8,128)S(1)}, u32[]{:S(2)}, u32[]{:S(2)}) collective-permute-start(f32[32,128,1]{1,0,2:T(8,128)S(1)} %get-tuple-element.49), channel_id=1, source_target_pairs={{2,0},{4,2},{6,4},{8,6},{10,8},{12,10},{14,12},{16,14},{18,16},{20... | collective-permute-start | bytes 49160 | tf_op jit(solution)/shard_map/ppermute | solution.py:17
  101.6 2.7 %copy.107 = f32[32,1,128]{2,0,1:T(8,128)S(1)} copy(f32[32,1,128]{1,0,2:T(8,128)} %slice.455) | data formatting | bytes 32768 | tf_op jit(solution)/shard_map/slice | solution.py:183
  105.2 20.9 %all_gather.7 = f32[32,1,2048]{2,0,1:T(8,128)S(1)} all-gather(f32[32,1,128]{2,0,1:T(8,128)S(1)} %copy.107), channel_id=1, replica_groups=mesh['lon'=16,'lat'=2] {'lon'}, dimensions={2}, use_global_device_ids=true | all-gather | bytes 278528 | tf_op jit(solution)/shard_map/all_gather | solution.py:90
  126.4 2.1 %fusion.76 = (f32[32,1,130]{1,0,2:T(8,128)S(1)}, f32[32,1,130]{1,0,2:T(8,128)}) fusion(f32[32,128,130]{1,0,2:T(8,128)S(1)} %pad_maximum_fusion.2), kind=kLoop, calls=%fused_computation.170 | loop fusion | bytes 66560 | tf_op jit(solution)/shard_map/slice | solution.py:11
  128.4 3.2 %copy.110 = f32[32,1,130]{2,0,1:T(8,128)S(1)} copy(f32[32,1,130]{1,0,2:T(8,128)} %get-tuple-element.43) | data formatting | bytes 33280 | tf_op jit(solution)/shard_map/slice | solution.py:12
  131.7 2.5 %collective-permute-start.7 = (f32[32,1,130]{2,0,1:T(8,128)S(1)}, f32[32,1,130]{2,0,1:T(8,128)S(1)}, u32[]{:S(2)}, u32[]{:S(2)}) collective-permute-start(f32[32,1,130]{2,0,1:T(8,128)S(1)} %copy.110), channel_id=1, source_target_pairs={{0,1},{1,0},{2,3},{3,2},{4,5},{5,4},{6,7},{7,6},{8,9},{9,8},{10,11... | collective-permute-start | bytes 49928 | tf_op jit(solution)/shard_map/ppermute | solution.py:15
  134.3 1.7 %copy.108 = f32[32,1,130]{2,0,1:T(8,128)S(1)} copy(f32[32,1,130]{1,0,2:T(8,128)S(1)} %get-tuple-element.42) | data formatting | bytes 33280 | tf_op jit(solution)/shard_map/slice | solution.py:11
  136.1 2.0 %copy.104 = f32[4,8,128,1]{3,2,1,0:T(8,128)} copy(f32[4,8,128,1]{2,1,0,3:T(8,128)S(1)} %bitcast.121) | data formatting | bytes 32768 | tf_op jit(solution)/shard_map/concatenate | solution.py:13
  138.1 2.0 %copy.106 = f32[4,8,128,1]{3,2,1,0:T(8,128)} copy(f32[4,8,128,1]{2,1,0,3:T(8,128)S(1)} %bitcast.122) | data formatting | bytes 32768 | tf_op jit(solution)/shard_map/concatenate | solution.py:13
  140.5 4.2 %fusion.28 = f32[4,8,128,128]{3,2,1,0:T(8,128)S(1)} fusion(f32[4,8,128,128]{3,2,1,0:T(8,128)S(1)} %copy-done.1, f32[4,8,1,128]{3,2,1,0:T(1,128)S(1)} %bitcast.124, f32[4,8,1,128]{3,2,1,0:T(1,128)S(1)} %bitcast.123, f32[4,8,128,1]{3,2,1,0:T(8,128)} %copy.106, f32[4,8,128,1]{3,2,1,0:T(8,128)} %copy.104, f32[8,128,128]{2,1,0:T(8,128)} %get-tuple-element.53, ...), kind=kLoop, calls=%fused_computation.42 | loop fusion | flops 8912896 | bytes 6357120 | tf_op jit(solution)/shard_map/add | solution.py:199
  145.9 1.4 slice_bitcast_fusion
  (152 shorter events, 28.4 us)
Async XLA Ops:
  7.2 3.5 %copy-start.9 = (f32[8,128,128]{2,1,0:T(8,128)S(1)}, f32[8,128,128]{2,1,0:T(8,128)}, u32[]{:S(2)}) copy-start(f32[8,128,128]{2,1,0:T(8,128)} %param.11) | copy-start | bytes 1572868
  7.2 4.5 %copy-start.10 = (f32[8,128,128]{2,1,0:T(8,128)S(1)}, f32[8,128,128]{2,1,0:T(8,128)}, u32[]{:S(2)}) copy-start(f32[8,128,128]{2,1,0:T(8,128)} %param.12) | copy-start | bytes 1572868
  7.2 5.4 %copy-start.11 = (f32[8,128,128]{2,1,0:T(8,128)S(1)}, f32[8,128,128]{2,1,0:T(8,128)}, u32[]{:S(2)}) copy-start(f32[8,128,128]{2,1,0:T(8,128)} %param.13) | copy-start | bytes 1572868
  7.2 76.2 %all-gather.2.cloned.1.call-start = ((), (), s32[]{:S(2)}) async-start(), calls=%async_computation | async-start | bytes 1705984 | tf_op jit(solution)/shard_map/all_gather | solution.py:90
  13.6 2.3 %copy-start.5 = (f32[8,128,128]{1,2,0:T(8,128)S(1)}, f32[8,128,128]{1,2,0:T(8,128)}, u32[]{:S(2)}) copy-start(f32[8,128,128]{1,2,0:T(8,128)} %copy.88) | copy-start | bytes 1572868
  13.6 2.4 %copy-start.6 = (f32[8,128,128]{1,2,0:T(8,128)S(1)}, f32[8,128,128]{1,2,0:T(8,128)}, u32[]{:S(2)}) copy-start(f32[8,128,128]{1,2,0:T(8,128)} %copy.89) | copy-start | bytes 1572868
  15.9 1.1 copy-start.30
  15.9 1.1 copy-start.31
  17.3 7.5 %collective-permute-start = (f32[42,128,3]{1,0,2:T(8,128)S(1)}, f32[42,128,3]{1,0,2:T(8,128)S(1)}, u32[]{:S(2)}, u32[]{:S(2)}) collective-permute-start(f32[42,128,3]{1,0,2:T(8,128)S(1)} %copy.92), channel_id=1, source_target_pairs={{0,2},{2,4},{4,6},{6,8},{8,10},{10,12},{12,14},{14,16},{16,18},{18... | collective-permute-start | bytes 193544 | tf_op jit(solution)/shard_map/ppermute | solution.py:15
  20.6 4.5 %collective-permute-start.1 = (f32[42,128,3]{1,0,2:T(8,128)}, f32[42,128,3]{1,0,2:T(8,128)}, u32[]{:S(2)}, u32[]{:S(2)}) collective-permute-start(f32[42,128,3]{1,0,2:T(8,128)} %copy.93), channel_id=1, source_target_pairs={{2,0},{4,2},{6,4},{8,6},{10,8},{12,10},{14,12},{16,14},{18,16},{20... | collective-permute-start | bytes 193544 | tf_op jit(solution)/shard_map/ppermute | solution.py:17
  32.5 2.0 %copy-start = (f32[8,128,128]{2,1,0:T(8,128)S(1)}, f32[8,128,128]{2,1,0:T(8,128)}, u32[]{:S(2)}) copy-start(f32[8,128,128]{2,1,0:T(8,128)} %copy.99) | copy-start | bytes 1572868
  34.5 1.5 copy-start.35
  35.2 6.0 %copy-start.12 = (f32[49,3,128]{2,1,0:T(4,128)}, f32[49,3,128]{2,1,0:T(4,128)S(1)}, u32[]{:S(2)}) copy-start(f32[49,3,128]{2,1,0:T(4,128)S(1)} %get-tuple-element.34) | copy-start | bytes 225796
  39.5 0.8 copy-start.3
  71.9 15.7 %collective-permute-start.2 = (f32[49,3,128]{2,1,0:T(4,128)}, f32[49,3,128]{2,1,0:T(4,128)S(1)}, u32[]{:S(2)}, u32[]{:S(2)}) collective-permute-start(f32[49,3,128]{2,1,0:T(4,128)} %copy-done.12), channel_id=1, source_target_pairs={{0,1},{2,3},{4,5},{6,7},{8,9},{10,11},{12,13},{14,15},{16,17},{18,... | collective-permute-start | bytes 225800 | tf_op jit(solution)/shard_map/ppermute | solution.py:15
  75.5 11.1 %collective-permute-start.3 = (f32[49,3,128]{2,1,0:T(4,128)}, f32[49,3,128]{2,1,0:T(4,128)}, u32[]{:S(2)}, u32[]{:S(2)}) collective-permute-start(f32[49,3,128]{2,1,0:T(4,128)} %get-tuple-element.35), channel_id=1, source_target_pairs={{1,0},{3,2},{5,4},{7,6},{9,8},{11,10},{13,12},{15,14},{17,16},{19,... | collective-permute-start | bytes 225800 | tf_op jit(solution)/shard_map/ppermute | solution.py:17
  77.0 9.6 %copy-start.34 = (f32[49]{0:T(128)S(1)}, f32[49]{0:T(128)}, u32[]{:S(2)}) copy-start(f32[49]{0:T(128)} %constant.14.clone.1) | copy-start | bytes 592
  96.6 7.6 %copy-start.2 = (f32[8,129,128]{2,1,0:T(8,128)S(1)}, f32[8,129,128]{2,1,0:T(8,128)}, u32[]{:S(2)}) copy-start(f32[8,129,128]{2,1,0:T(8,128)} %get-tuple-element.26) | copy-start | bytes 1585156
  98.6 27.6 %collective-permute-start.4 = (f32[32,128,1]{1,0,2:T(8,128)S(1)}, f32[32,128,1]{1,0,2:T(8,128)S(1)}, u32[]{:S(2)}, u32[]{:S(2)}) collective-permute-start(f32[32,128,1]{1,0,2:T(8,128)S(1)} %get-tuple-element.49), channel_id=1, source_target_pairs={{2,0},{4,2},{6,4},{8,6},{10,8},{12,10},{14,12},{16,14},{18,16},{20... | collective-permute-start | bytes 49160 | tf_op jit(solution)/shard_map/ppermute | solution.py:17
  101.6 24.6 %collective-permute-start.5 = (f32[32,128,1]{1,0,2:T(8,128)S(1)}, f32[32,128,1]{1,0,2:T(8,128)S(1)}, u32[]{:S(2)}, u32[]{:S(2)}) collective-permute-start(f32[32,128,1]{1,0,2:T(8,128)S(1)} %get-tuple-element.48), channel_id=1, source_target_pairs={{0,2},{2,4},{4,6},{6,8},{8,10},{10,12},{12,14},{14,16},{16,18},{18... | collective-permute-start | bytes 49160 | tf_op jit(solution)/shard_map/ppermute | solution.py:15
  131.7 8.4 %collective-permute-start.7 = (f32[32,1,130]{2,0,1:T(8,128)S(1)}, f32[32,1,130]{2,0,1:T(8,128)S(1)}, u32[]{:S(2)}, u32[]{:S(2)}) collective-permute-start(f32[32,1,130]{2,0,1:T(8,128)S(1)} %copy.110), channel_id=1, source_target_pairs={{0,1},{1,0},{2,3},{3,2},{4,5},{5,4},{6,7},{7,6},{8,9},{9,8},{10,11... | collective-permute-start | bytes 49928 | tf_op jit(solution)/shard_map/ppermute | solution.py:15
  136.0 4.2 %copy-start.33 = (f32[32]{0:T(128)S(1)}, f32[32]{0:T(128)}, u32[]{:S(2)}) copy-start(f32[32]{0:T(128)} %constant.15.clone.1) | copy-start | bytes 388
  136.0 4.3 %copy-start.1 = (f32[4,8,128,128]{3,2,1,0:T(8,128)S(1)}, f32[4,8,128,128]{3,2,1,0:T(8,128)}, u32[]{:S(2)}) copy-start(f32[4,8,128,128]{3,2,1,0:T(8,128)} %fusion.37) | copy-start | bytes 6291460
  136.0 4.3 %copy-start.4 = (f32[8,128,128]{2,1,0:T(8,128)S(1)}, f32[8,128,128]{2,1,0:T(8,128)}, u32[]{:S(2)}) copy-start(f32[8,128,128]{2,1,0:T(8,128)} %copy.102) | copy-start | bytes 1572868
  136.0 4.3 %copy-start.32 = (f32[4,8]{1,0:T(4,128)S(1)}, f32[4,8]{1,0:T(4,128)}, u32[]{:S(2)}) copy-start(f32[4,8]{1,0:T(4,128)} %param.18) | copy-start | bytes 388
  136.0 4.2 %collective-permute-start.6 = (f32[32,1,130]{2,0,1:T(8,128)S(1)}, f32[32,1,130]{2,0,1:T(8,128)S(1)}, u32[]{:S(2)}, u32[]{:S(2)}) collective-permute-start(f32[32,1,130]{2,0,1:T(8,128)S(1)} %copy.108), channel_id=1, source_target_pairs={{1,0},{0,1},{3,2},{2,3},{5,4},{4,5},{7,6},{6,7},{9,8},{8,9},{11,10... | collective-permute-start | bytes 49928 | tf_op jit(solution)/shard_map/ppermute | solution.py:17
  140.3 4.4 %copy-start.7 = (f32[128,128]{1,0:T(8,128)S(1)}, f32[128,128]{1,0:T(8,128)}, u32[]{:S(2)}) copy-start(f32[128,128]{1,0:T(8,128)} %copy.120) | copy-start | bytes 196612
  140.3 4.4 %copy-start.8 = (f32[128,128]{1,0:T(8,128)S(1)}, f32[128,128]{1,0:T(8,128)}, u32[]{:S(2)}) copy-start(f32[128,128]{1,0:T(8,128)} %copy.132) | copy-start | bytes 196612
  140.3 4.4 %copy-start.13 = (f32[128,128]{1,0:T(8,128)S(1)}, f32[128,128]{1,0:T(8,128)}, u32[]{:S(2)}) copy-start(f32[128,128]{1,0:T(8,128)} %copy.113) | copy-start | bytes 196612
  140.3 4.4 %copy-start.14 = (f32[128,128]{1,0:T(8,128)S(1)}, f32[128,128]{1,0:T(8,128)}, u32[]{:S(2)}) copy-start(f32[128,128]{1,0:T(8,128)} %copy.114) | copy-start | bytes 196612
  140.3 4.4 %copy-start.15 = (f32[128,128]{1,0:T(8,128)S(1)}, f32[128,128]{1,0:T(8,128)}, u32[]{:S(2)}) copy-start(f32[128,128]{1,0:T(8,128)} %copy.116) | copy-start | bytes 196612
  140.3 4.4 %copy-start.16 = (f32[128,128]{1,0:T(8,128)S(1)}, f32[128,128]{1,0:T(8,128)}, u32[]{:S(2)}) copy-start(f32[128,128]{1,0:T(8,128)} %copy.117) | copy-start | bytes 196612
  140.3 4.4 %copy-start.17 = (f32[128,128]{1,0:T(8,128)S(1)}, f32[128,128]{1,0:T(8,128)}, u32[]{:S(2)}) copy-start(f32[128,128]{1,0:T(8,128)} %copy.119) | copy-start | bytes 196612
  140.3 4.4 %copy-start.18 = (f32[128,128]{1,0:T(8,128)S(1)}, f32[128,128]{1,0:T(8,128)}, u32[]{:S(2)}) copy-start(f32[128,128]{1,0:T(8,128)} %copy.122) | copy-start | bytes 196612
  140.3 4.4 %copy-start.19 = (f32[128,128]{1,0:T(8,128)S(1)}, f32[128,128]{1,0:T(8,128)}, u32[]{:S(2)}) copy-start(f32[128,128]{1,0:T(8,128)} %copy.123) | copy-start | bytes 196612
  140.4 4.4 %copy-start.20 = (f32[128,128]{1,0:T(8,128)S(1)}, f32[128,128]{1,0:T(8,128)}, u32[]{:S(2)}) copy-start(f32[128,128]{1,0:T(8,128)} %copy.125) | copy-start | bytes 196612
  140.4 4.4 %copy-start.21 = (f32[128,128]{1,0:T(8,128)S(1)}, f32[128,128]{1,0:T(8,128)}, u32[]{:S(2)}) copy-start(f32[128,128]{1,0:T(8,128)} %copy.128) | copy-start | bytes 196612
  140.4 4.4 %copy-start.22 = (f32[128,128]{1,0:T(8,128)S(1)}, f32[128,128]{1,0:T(8,128)}, u32[]{:S(2)}) copy-start(f32[128,128]{1,0:T(8,128)} %copy.129) | copy-start | bytes 196612
  140.4 4.4 %copy-start.23 = (f32[128,128]{1,0:T(8,128)S(1)}, f32[128,128]{1,0:T(8,128)}, u32[]{:S(2)}) copy-start(f32[128,128]{1,0:T(8,128)} %copy.131) | copy-start | bytes 196612
  140.4 4.4 %copy-start.24 = (f32[128,128]{1,0:T(8,128)S(1)}, f32[128,128]{1,0:T(8,128)}, u32[]{:S(2)}) copy-start(f32[128,128]{1,0:T(8,128)} %copy.115) | copy-start | bytes 196612
  140.4 4.4 %copy-start.25 = (f32[128,128]{1,0:T(8,128)S(1)}, f32[128,128]{1,0:T(8,128)}, u32[]{:S(2)}) copy-start(f32[128,128]{1,0:T(8,128)} %copy.118) | copy-start | bytes 196612
  140.4 4.4 %copy-start.26 = (f32[128,128]{1,0:T(8,128)S(1)}, f32[128,128]{1,0:T(8,128)}, u32[]{:S(2)}) copy-start(f32[128,128]{1,0:T(8,128)} %copy.121) | copy-start | bytes 196612
  140.4 4.4 %copy-start.27 = (f32[128,128]{1,0:T(8,128)S(1)}, f32[128,128]{1,0:T(8,128)}, u32[]{:S(2)}) copy-start(f32[128,128]{1,0:T(8,128)} %copy.124) | copy-start | bytes 196612
  140.4 4.4 %copy-start.28 = (f32[128,128]{1,0:T(8,128)S(1)}, f32[128,128]{1,0:T(8,128)}, u32[]{:S(2)}) copy-start(f32[128,128]{1,0:T(8,128)} %copy.127) | copy-start | bytes 196612
  140.4 4.4 %copy-start.29 = (f32[128,128]{1,0:T(8,128)S(1)}, f32[128,128]{1,0:T(8,128)}, u32[]{:S(2)}) copy-start(f32[128,128]{1,0:T(8,128)} %copy.130) | copy-start | bytes 196612
Sparse Core Ops, SparseCore 0:
  36.1 41.2 all-gather.1
where the time goes:
time: 156 us; the launch traced here: 154 us
  local copies, waits for them, and re-layouts  78.3 us (50%)
  other arithmetic  26.2 us (17%)
  blocking collectives  20.9 us (13%)
  between operations  15 us (10%)
  starting transfers between devices  13.3 us (9%)
    all_gather x1, blocking collectives, fold_rows(): whole_rows = lax.all_gather(block_rows, 'lon', axis=2, tiled=True)  20.9 us
    div x14, local copies, waits for them, and re-layouts, vertical_solve(): factors.append(downward / divisor)  18.2 us
    unnamed x84, local copies, waits for them, and re-layouts  9.52 us
    sub x7, local copies, waits for them, and re-layouts, vertical_solve(): divisor = divisor - upward * factors[layer_index - 1]  9.41 us
    ppermute x4, starting transfers between devices, extended_2(): lax.ppermute(tail, axis, [(i, (i + 1) % count) for i in range(ends)])  8.74 us
    slice x2, local copies, waits for them, and re-layouts, shards(): flat_fields[:, parallel_total - 1:, :]  4.61 us
    ppermute x4, starting transfers between devices, extended_2(): lax.ppermute(head, axis, [((i + 1) % count, i) for i in range(ends)])  4.56 us
    slice x3, local copies, waits for them, and re-layouts, extended_2(): head = lax.slice_in_dim(cells, 0, width, axis=dim)  4.43 us
  transfers between devices with their start and end apart: 9, of which 1 were waited for; matrix products, arithmetic and copies ran while one was open for 39% of the time, Pallas kernels for 0%

commit v1 on v0

v1 whole, which is shorter than its diff:
```python
import jax
import jax.numpy as jnp
from jax import lax
from jax.experimental import pallas as pl
from jax.experimental.pallas import tpu as pltpu
from jax.sharding import PartitionSpec as P

LANES = 128
SP, VM, VMP, WET, WETP, MY, MYP, WX, WXP, PLANES = 32, 34, 42, 43, 51, 52, 53, 54, 62, 63
WIDE, THIN = 34, 20
MSG = WIDE * 4 + THIN * 2
VMEM_LIMIT = 56 * 1024 * 1024


def lane_of(rows):
    return lax.broadcasted_iota(jnp.int32, (rows, LANES), 1)


def roll(x, s):
    if isinstance(s, int):
        s = s % LANES
        if s == 0:
            return x
    return pltpu.roll(x, s, 1)


def shifted(q, halo, s, lane):
    if s > 0:
        return roll(jnp.where(lane < s, halo, q), -s)
    return roll(jnp.where(lane >= LANES + s, halo, q), -s)


def group_roll(x, g):
    return pltpu.roll(x, (LANES - 8 * g) % LANES, 1)


def coefs(courant, opening):
    a = jnp.abs(courant)
    ak = a * (1.0 - (2.0 / 3.0) * a)
    cc = courant * opening
    return (
        cc * (1.0 - 0.5 * a - 1.5 * ak),
        cc * (0.5 * a - 1.5 * ak),
        cc * (3.0 * ak),
        courant >= 0.0,
    )


def edge(qm, q0, q1, q2):
    return (7.0 / 12.0) * (q0 + q1) - (1.0 / 12.0) * (qm + q2)


def flux(cf, em, e0, e1, q0, q1):
    a0, a1, a2, up = cf
    return a0 * e0 + a1 * jnp.where(up, em, e1) + a2 * jnp.where(up, q0, q1)


def pack_kernel(t_ref, s_ref, u_ref, v_ref, wet_ref, mx_ref, my_ref, c_ref):
    rows = 32
    total = t_ref.shape[1]
    lane = lane_of(rows)
    group = ((lane + 4) % LANES) // 8

    def chunk(i, carry):
        r = pl.ds(pl.multiple_of(i * rows, rows), rows)
        wets = [wet_ref[k, r, :].astype(jnp.float32) for k in range(8)]
        for a, pair in enumerate(((t_ref, s_ref), (u_ref, v_ref))):
            acc = jnp.zeros((rows, LANES), jnp.float32)
            for h, ref in enumerate(pair):
                for k in range(8):
                    g = 8 * h + k
                    acc = jnp.where(group == g, roll(ref[k, r, :] * wets[k], 8 * g), acc)
            c_ref[a, r, :] = acc
        acc = jnp.zeros((rows, LANES), jnp.float32)
        for g, x in enumerate(wets + [mx_ref[r, :], my_ref[r, :]]):
            acc = jnp.where(group == g, roll(x, 8 * g), acc)
        c_ref[2, r, :] = acc
        return carry

    lax.fori_loop(0, total // rows, chunk, 0)


def packed_x(c_ref, l_ref, r_ref, T, r, tr, rows):
    lane = lane_of(rows)
    low = lane % 8 < 4
    place = (lane + 4) % LANES
    half = place < 64
    group = place // 8
    parts = []
    for right in (True, False):
        near, far = (c_ref, r_ref) if right else (l_ref, c_ref)
        e = [jnp.where(low, far[a, r, :], near[a, r, :]) for a in range(3)]

        def both(x, first):
            y = pltpu.roll(x, 64, 1)
            return jnp.where(half, x, y) if first else jnp.where(half, y, x)

        def spread(x, g):
            x = jnp.where(group == g, x, 0.0)
            for s in (8, 16, 32, 64):
                x = x + pltpu.roll(x, s, 1)
            return x

        u, v, wet = both(e[1], True), both(e[1], False), both(e[2], True)
        mx, my = spread(e[2], 8), spread(e[2], 9)
        um = u * mx
        opening = wet * roll(wet, -1)
        weight = 0.5 * (mx + roll(mx, -1)) * opening
        cf = coefs(0.5 * (um + roll(um, -1)), opening)
        starred, fluxes = [], []
        for a in range(2):
            q = e[a]
            q1 = roll(q, -1)
            ed = edge(roll(q, 1), q, q1, roll(q, -2))
            f = flux(cf, roll(ed, 1), ed, roll(ed, -1), q, q1)
            starred.append(q + roll(f, 1) - f)
            fluxes.append(f)
        parts.append((starred, fluxes, weight, v * my, wet, my))
    (rs, _, _, rvm, rwet, rmy), (ls, lf, lw, lvm, lwet, lmy) = parts
    for a in range(2):
        T[SP + a, tr, :] = jnp.where(low, rs[a], ls[a])
    T[VMP, tr, :] = jnp.where(low, rvm, lvm)
    T[WETP, tr, :] = jnp.where(low, rwet, lwet)
    T[MYP, tr, :] = jnp.where(low, rmy, lmy)
    T[WXP, tr, :] = lw
    return lf


def x_phase(fields, wet_ref, mx_ref, my_ref, c_ref, l_ref, r_ref, T, H, r, tr, rows):
    lane = lane_of(rows)
    low = lane % 8 < 4
    lf = packed_x(c_ref, l_ref, r_ref, T, r, tr, rows)
    for a in range(3):
        H[a] = jnp.where(low, r_ref[a, r, :], l_ref[a, r, :])
    for a in range(2):
        H[3 + a] = lf[a]
    mx = mx_ref[r, :]
    my = my_ref[r, :]
    T[MY, tr, :] = my
    mxh = group_roll(H[2], 8)
    mx1 = shifted(mx, mxh, 1, lane)

    def level(k, carry):
        wet = wet_ref[k, r, :].astype(jnp.float32)
        T[WET + k, tr, :] = wet
        hwet = group_roll(H[2], k)
        opening = wet * shifted(wet, hwet, 1, lane)
        T[WX + k, tr, :] = 0.5 * (mx + mx1) * opening
        hu = group_roll(H[1], k)
        um = fields[2][k, r, :] * wet * mx
        cf = coefs(0.5 * (um + shifted(um, hu * mxh, 1, lane)), opening)
        for f in range(4):
            q = fields[f][k, r, :] * wet
            if f == 3:
                T[VM + k, tr, :] = q * my
            g = 8 * (f % 2) + k
            h = hu if f == 2 else group_roll(H[f // 2], g)
            qm, q1, q2 = (shifted(q, h, s, lane) for s in (-1, 1, 2))
            ed = edge(qm, q, q1, q2)
            hm1, h1 = roll(h, 1), roll(h, -1)
            m2, p2 = hm1, roll(h, -2)
            em_fix = edge(m2, h, roll(q, -1), roll(q, -2))
            e1_fix = edge(roll(q, 1), h, h1, p2)
            em = roll(jnp.where(lane == LANES - 1, em_fix, ed), 1)
            e1 = roll(jnp.where(lane == 0, e1_fix, ed), -1)
            fl = flux(cf, em, ed, e1, q, q1)
            flm = roll(jnp.where(lane == LANES - 1, group_roll(H[3 + f // 2], g), fl), 1)
            T[8 * f + k, tr, :] = q + flm - fl
        return carry

    lax.fori_loop(0, 8, level, 0)


def face_y(T, vm, wet, my, WY, kw, r0, rows):
    r, r1 = pl.ds(r0, rows), pl.ds(r0 + 1, rows)
    opening = T[wet, r, :] * T[wet, r1, :]
    if WY is not None:
        WY[kw, r, :] = 0.5 * (T[my, r, :] + T[my, r1, :]) * opening
    return coefs(0.5 * (T[vm, r, :] + T[vm, r1, :]), opening)


def y_advect(T, E, F, A, WY, planes, vm, wet, my, kw, chunks):
    for r0, rows in chunks:
        for n, p in enumerate(planes):
            E[n, pl.ds(r0, rows), :] = edge(*(T[p, pl.ds(r0 + s, rows), :] for s in (-1, 0, 1, 2)))
    for r0, rows in chunks:
        cf = face_y(T, vm, wet, my, WY, kw, r0, rows)
        for n, p in enumerate(planes):
            em, e0, e1 = (E[n, pl.ds(r0 + s, rows), :] for s in (-1, 0, 1))
            q0, q1 = (T[p, pl.ds(r0 + s, rows), :] for s in (0, 1))
            F[n, pl.ds(r0, rows), :] = flux(cf, em, e0, e1, q0, q1)
    for r0, rows in chunks:
        for n, p in enumerate(planes):
            r = pl.ds(r0, rows)
            A[p, r, :] = T[p, r, :] + F[n, pl.ds(r0 - 1, rows), :] - F[n, r, :]


def y_phase(T, E, F, A, WY, chunks):
    y_advect(T, E, F, A, None, (SP, SP + 1), VMP, WETP, MYP, 0, chunks)

    def level(k, carry):
        y_advect(T, E, F, A, WY, tuple(8 * f + k for f in range(4)), VM + k, WET + k, MY, k, chunks)
        return carry

    lax.fori_loop(0, 8, level, 0)


def finish(T, A, WY, idf_ref, coef_ref, outs, t0, o0, rows):
    lane = lane_of(rows)
    r, rp, rm = pl.ds(t0, rows), pl.ds(t0 + 1, rows), pl.ds(t0 - 1, rows)
    o = pl.ds(o0, rows)
    wet = [T[WET + k, r, :] for k in range(8)]
    wxp = T[WXP, r, :]
    ap = [A[SP + a, r, :] for a in range(2)]
    up = None
    reduced, factors = [], []
    for k in range(8):
        wx = T[WX + k, r, :]
        wxm = roll(jnp.where(lane == LANES - 1, roll(wxp, -8 * k), wx), 1)
        wy, wym = WY[k, r, :], WY[k, rm, :]
        down = idf_ref[k, o, :] * wet[k] * wet[k + 1] if k < 7 else None
        divisor = 1.0
        if up is not None:
            divisor = divisor + up * (1.0 - factors[-1])
        if down is not None:
            divisor = divisor + down
        inv = 1.0 / divisor
        row = []
        for f in range(4):
            p = 8 * f + k
            a = A[p, r, :]
            h = roll(ap[f // 2], -8 * (8 * (f % 2) + k))
            a1 = roll(jnp.where(lane == 0, h, a), -1)
            am = roll(jnp.where(lane == LANES - 1, h, a), 1)
            lap = wx * (a1 - a) - wxm * (a - am) + wy * (A[p, rp, :] - a) - wym * (a - A[p, rm, :])
            d = a + coef_ref[f, k] * lap
            if up is not None:
                d = d + up * reduced[-1][f]
            row.append(d * inv)
        reduced.append(row)
        if down is not None:
            factors.append(down * inv)
        up = down
    x = reduced[7]
    for k in range(7, -1, -1):
        if k < 7:
            x = [reduced[k][f] + factors[k] * x[f] for f in range(4)]
        for f in range(4):
            outs[f][k, o, :] = x[f] * wet[k]


def edge_rows_kernel(t, s, u, v, wet, mx, my, c, l, r, msg, T, H):
    x_phase((t, s, u, v), wet, mx, my, c, l, r, T, H, pl.ds(0, 8), pl.ds(0, 8), 8)
    side = pl.program_id(0)

    @pl.when(side == 0)
    def _():
        for p in range(WIDE):
            msg[0, 4 * p : 4 * p + 4, :] = T[p, 0:4, :]
        for p in range(THIN):
            msg[0, 4 * WIDE + 2 * p : 4 * WIDE + 2 * p + 2, :] = T[WIDE + p, 0:2, :]

    @pl.when(side == 1)
    def _():
        for p in range(WIDE):
            msg[0, 4 * p : 4 * p + 4, :] = T[p, 4:8, :]
        for p in range(THIN):
            msg[0, 4 * WIDE + 2 * p : 4 * WIDE + 2 * p + 2, :] = T[WIDE + p, 6:8, :]


def interior_kernel(coef, t, s, u, v, wet, mx, my, c, l, r, idf, o0, o1, o2, o3, bnd, T, H, E, F, A, WY):
    total = t.shape[1]
    rows = 32

    def chunk(i, carry):
        a = pl.multiple_of(i * rows, rows)
        x_phase((t, s, u, v), wet, mx, my, c, l, r, T, H, pl.ds(a, rows), pl.ds(pl.multiple_of(a + 8, 8), rows), rows)
        return carry

    lax.fori_loop(0, total // rows, chunk, 0)
    bnd[:, 0:16, :] = T[:, 8:24, :]
    bnd[:, 16:32, :] = T[:, total - 8 : total + 8, :]
    y_phase(T, E, F, A, WY, tuple((8 + i, rows) for i in range(0, total, rows)))

    def tile(i, carry):
        a = pl.multiple_of(i * 8, 8)
        finish(T, A, WY, idf, coef, (o0, o1, o2, o3), a + 8, a, 8)
        return carry

    lax.fori_loop(1, total // 8 - 1, tile, 0)


def border_kernel(place, coef, idf, bnd, from_south, from_north, fold, i0, i1, i2, i3, o0, o1, o2, o3, T, E, F, A, WY, R):
    side = pl.program_id(0)

    @pl.when(side == 0)
    def _():
        T[:, 16:32, :] = bnd[...]
        for p in range(WIDE):
            T[p, 12:16, :] = from_south[4 * p : 4 * p + 4, :]
        for p in range(THIN):
            n = 4 * WIDE + 2 * p
            T[WIDE + p, 14:16, :] = from_south[n : n + 2, :]

    @pl.when(side == 1)
    def _():
        T[:, 8:24, :] = bnd[...]

    @pl.when((side == 1) & (place[1] == 0))
    def _():
        for p in range(WIDE):
            T[p, 24:28, :] = from_north[4 * p : 4 * p + 4, :]
        for p in range(THIN):
            n = 4 * WIDE + 2 * p
            T[WIDE + p, 24:26, :] = from_north[n : n + 2, :]

    @pl.when((side == 1) & (place[1] == 1))
    def _():
        x = fold[0]
        lane = lane_of(MSG)
        row = lax.broadcasted_iota(jnp.int32, (MSG, LANES), 0)
        back = jnp.take_along_axis(x, LANES - 1 - lane, axis=1)
        swap = jnp.where(lane % 8 == 0, roll(x, 1), roll(x, -1))
        w = 4 * WIDE
        packed = (
            ((row >= 4 * SP) & (row < w))
            | ((row >= w + 2 * (VMP - WIDE)) & (row < w + 2 * (WET - WIDE)))
            | ((row >= w + 2 * (WETP - WIDE)) & (row < w + 2 * (MY - WIDE)))
            | (row >= w + 2 * (MYP - WIDE))
        )
        minus = (
            ((row >= 64) & (row < 4 * SP))
            | ((row >= 4 * SP + 4) & (row < w))
            | ((row >= w) & (row < w + 2 * (WET - WIDE)))
        )
        y = jnp.where(packed, swap, back)
        R[...] = jnp.where(minus, -y, y)
        for p in range(WIDE):
            for i in range(4):
                T[p, 24 + i : 25 + i, :] = R[4 * p + 3 - i : 4 * p + 4 - i, :]
        for p in range(THIN):
            for i in range(2):
                n = w + 2 * p + 1 - i
                T[WIDE + p, 24 + i : 25 + i, :] = R[n : n + 1, :]

    y_phase(T, E, F, A, WY, ((8, 24),))
    finish(T, A, WY, idf, coef, (o0, o1, o2, o3), 16, 0, 8)


def vspec():
    return pl.BlockSpec(memory_space=pltpu.VMEM)


def sspec():
    return pl.BlockSpec(memory_space=pltpu.SMEM)


def shards(heat, salt, east, north, water, mx, my, idf, spreading, mirror):
    f32 = jnp.float32
    rows_total = heat.shape[1]
    last = rows_total // 8 - 1
    params = pltpu.CompilerParams(vmem_limit_bytes=VMEM_LIMIT)
    fields = (heat, salt, east, north)
    cols = pl.pallas_call(
        pack_kernel,
        out_shape=jax.ShapeDtypeStruct((3, rows_total, LANES), f32),
        in_specs=[vspec()] * 7,
        out_specs=vspec(),
        compiler_params=params,
    )(*fields, water, mx, my)
    n = lax.axis_size("lon")
    left = lax.ppermute(cols, "lon", [(i, (i + 1) % n) for i in range(n)])
    right = lax.ppermute(cols, "lon", [((i + 1) % n, i) for i in range(n)])

    deep = pl.BlockSpec((8, 8, LANES), lambda i: (0, last * i, 0))
    flat = pl.BlockSpec((8, LANES), lambda i: (last * i, 0))
    three = pl.BlockSpec((3, 8, LANES), lambda i: (0, last * i, 0))
    msg = pl.pallas_call(
        edge_rows_kernel,
        out_shape=jax.ShapeDtypeStruct((2, MSG, LANES), f32),
        grid=(2,),
        in_specs=[deep] * 5 + [flat] * 2 + [three] * 3,
        out_specs=pl.BlockSpec((1, MSG, LANES), lambda i: (i, 0, 0)),
        scratch_shapes=[pltpu.VMEM((PLANES, 8, LANES), f32), pltpu.VMEM((5, 8, LANES), f32)],
        compiler_params=params,
    )(*fields, water, mx, my, cols, left, right)
    m = lax.axis_size("lat")
    from_south = lax.ppermute(msg[1], "lat", [(i, i + 1) for i in range(m - 1)])
    from_north = lax.ppermute(msg[0], "lat", [(i + 1, i) for i in range(m - 1)])
    gathered = lax.all_gather(msg[1], "lon", axis=0)

    tall = rows_total + 16
    out = jax.ShapeDtypeStruct((8, rows_total, LANES), f32)
    results = pl.pallas_call(
        interior_kernel,
        out_shape=[out] * 4 + [jax.ShapeDtypeStruct((PLANES, 32, LANES), f32)],
        in_specs=[sspec()] + [vspec()] * 11,
        out_specs=[vspec()] * 5,
        scratch_shapes=[
            pltpu.VMEM((PLANES, tall, LANES), f32),
            pltpu.VMEM((5, 32, LANES), f32),
            pltpu.VMEM((4, tall, LANES), f32),
            pltpu.VMEM((4, tall, LANES), f32),
            pltpu.VMEM((WIDE, tall, LANES), f32),
            pltpu.VMEM((8, tall, LANES), f32),
        ],
        compiler_params=params,
        cost_estimate=pl.CostEstimate(flops=60_000_000, bytes_accessed=40_000_000, transcendentals=0),
    )(spreading, *fields, water, mx, my, cols, left, right, idf)
    bnd = results[4]

    tile = mirror[0] // LANES
    northern = (lax.axis_index("lat") == m - 1).astype(jnp.int32)
    place = jnp.stack([tile, northern])
    anyspec = pl.BlockSpec(memory_space=pl.ANY)
    whole = pl.BlockSpec((MSG, LANES), lambda i, pf: (0, 0))
    outs = pl.pallas_call(
        border_kernel,
        out_shape=[out] * 4,
        grid_spec=pltpu.PrefetchScalarGridSpec(
            num_scalar_prefetch=1,
            grid=(2,),
            in_specs=[
                sspec(),
                pl.BlockSpec((7, 8, LANES), lambda i, pf: (0, last * i, 0)),
                pl.BlockSpec((PLANES, 16, LANES), lambda i, pf: (0, i, 0)),
                whole,
                whole,
                pl.BlockSpec((1, MSG, LANES), lambda i, pf: (pf[0], 0, 0)),
            ]
            + [anyspec] * 4,
            out_specs=[pl.BlockSpec((8, 8, LANES), lambda i, pf: (0, last * i, 0))] * 4,
            scratch_shapes=[
                pltpu.VMEM((PLANES, 40, LANES), f32),
                pltpu.VMEM((4, 40, LANES), f32),
                pltpu.VMEM((4, 40, LANES), f32),
                pltpu.VMEM((WIDE, 40, LANES), f32),
                pltpu.VMEM((8, 40, LANES), f32),
                pltpu.VMEM((MSG, LANES), f32),
            ],
        ),
        input_output_aliases={7 + i: i for i in range(4)},
        compiler_params=params,
    )(place, spreading, idf, bnd, from_south, from_north, gathered, *results[:4])
    return tuple(outs)


def solution(mesh):
    deep = P(None, "lat", "lon")
    flat = P("lat", "lon")
    return jax.shard_map(
        shards,
        mesh=mesh,
        in_specs=(deep,) * 5 + (flat, flat, deep, P(), P("lon")),
        out_specs=(deep,) * 4,
        check_vma=False,
    )
```

time: 156 us -> 81.9 us (0.53)
  local copies, waits for them, and re-layouts: 78.3 us -> 2.27 us
  Pallas kernels: 0 us -> 42.2 us
  other arithmetic: 26.2 us -> 0.64 us
  blocking collectives: 20.9 us -> 0 us
  waiting for transfers between devices: 0.24 us -> 15 us
  starting transfers between devices: 13.3 us -> 7.08 us
    pallas_call x0 -> x4, Pallas kernels: none -> 42.2 us  [the longest x1 27.2 us: shards(): pl.pallas_call(interior_kernel, out_shape=[out] * 4 + [jax.ShapeDtypeStru...]
    all_gather x1 -> x0, blocking collectives: 20.9 us -> none  [fold_rows(): whole_rows = lax.all_gather(block_rows, 'lon', axis=2, tiled=True)]
    slice x15 -> x1, local copies, waits for them, and re-layouts: 20 us -> 1.58 us  [shards(): from_south = lax.ppermute(msg[1], 'lat', [(i, i + 1) for i in range(m - 1)])]
    div x14 -> x0, local copies, waits for them, and re-layouts: 18.2 us -> none  [vertical_solve(): factors.append(downward / divisor)]
    all_gather x1, waiting for transfers between devices: 0.01 us -> 9.92 us  [shards(): gathered = lax.all_gather(msg[1], 'lon', axis=0)]
    sub x7 -> x0, local copies, waits for them, and re-layouts: 9.41 us -> none  [vertical_solve(): divisor = divisor - upward * factors[layer_index - 1]]
    unnamed x84 -> x10, local copies, waits for them, and re-layouts: 9.52 us -> 0.69 us
    add x3 -> x0, other arithmetic: 7.93 us -> none  [the longest x1 4.24 us: shards(): diffused = advected + spreading_coefficient[:, :, None, None] * laplacian]
  transfers between devices with their start and end apart: 9 -> 5, of which waited for: 1 -> 3; matrix products, arithmetic and copies ran while one was open for 39% -> 1% of each run, Pallas kernels for 0% -> 33%
where the time goes in v1:
time: 81.9 us; the launch traced here: 81.4 us
  Pallas kernels  42.2 us (52%)
  waiting for transfers between devices  15 us (18%)
  between operations  14.2 us (17%)
  starting transfers between devices  7.08 us (9%)
  local copies, waits for them, and re-layouts  2.27 us (3%)
    pallas_call x1, Pallas kernels, shards(): pl.pallas_call(interior_kernel, out_shape=[out] * 4 + [jax.ShapeDtypeStru...  27.2 us
    all_gather x1, waiting for transfers between devices, shards(): gathered = lax.all_gather(msg[1], 'lon', axis=0)  9.92 us
    pallas_call x1, Pallas kernels, shards(): pl.pallas_call(edge_rows_kernel, out_shape=jax.ShapeDtypeStruct((2, MSG,...  7.63 us
    pallas_call x1, Pallas kernels, shards(): pl.pallas_call(border_kernel, out_shape=[out] * 4, grid_spec=pltpu.Prefet...  4.03 us
    ppermute x1, waiting for transfers between devices, shards(): right = lax.ppermute(cols, 'lon', [((i + 1) % n, i) for i in range(n)])  3.56 us
    pallas_call x1, Pallas kernels, shards(): pl.pallas_call(pack_kernel, out_shape=jax.ShapeDtypeStruct((3, rows_total...  3.33 us
    ppermute x1, starting transfers between devices, shards(): from_south = lax.ppermute(msg[1], 'lat', [(i, i + 1) for i in range(m - 1)])  3.15 us
    ppermute x1, starting transfers between devices, shards(): left = lax.ppermute(cols, 'lon', [(i, (i + 1) % n) for i in range(n)])  2.55 us
  transfers between devices with their start and end apart: 5, of which 3 were waited for; matrix products, arithmetic and copies ran while one was open for 1% of the time, Pallas kernels for 33%

profile of v1, /device:TPU:1, one launch (start us, length us, event | category | flops | bytes accessed | tf_op | source)
XLA Modules:
  0.0 81.4 jit_solution(9036835628464974548)
XLA Ops:
  7.2 0.0 all-gather.2.cloned.1.call-start
  7.2 3.3 %shard_map.129.c = f32[3,128,128]{2,1,0:T(8,128)} custom-call(f32[8,128,128]{2,1,0:T(8,128)} %t.3, f32[8,128,128]{2,1,0:T(8,128)} %s.3, f32[8,128,128]{2,1,0:T(8,128)} %u.3, f32[8,128,128]{2,1,0:T(8,128)} %v.3, s32[8,128,128]{2,1,0:T(8,128)} %wet.3, f32[128,128]{1,0:T(8,128)} %mx.3, f32[128,128]{1,0:T(8,128)} %my.3), custom_call_target="tpu_custom_call" | custom-call | tf_op jit(solution)/shard_map/pallas_call | solution.py:364
  10.5 0.0 copy-start.4
  10.5 0.1 collective-permute-start.1
  10.6 2.5 %collective-permute-start = (f32[3,128,128]{2,1,0:T(8,128)}, f32[3,128,128]{2,1,0:T(8,128)S(1)}, u32[]{:S(2)}, u32[]{:S(2)}) collective-permute-start(f32[3,128,128]{2,1,0:T(8,128)} %shard_map.129.c), channel_id=1, source_target_pairs={{0,2},{2,4},{4,6},{6,8},{8,10},{10,12},{12,14},{14,16},{16,18},{18... | collective-permute-start | bytes 589832 | tf_op jit(solution)/shard_map/ppermute | solution.py:372
  13.2 3.6 %collective-permute-done.1.r = f32[3,128,128]{2,1,0:T(8,128)S(1)} collective-permute-done((f32[3,128,128]{2,1,0:T(8,128)}, f32[3,128,128]{2,1,0:T(8,128)S(1)}, u32[]{:S(2)}, u32[]{:S(2)}) %collective-permute-start.1) | collective-permute-done | bytes 196640 | tf_op jit(solution)/shard_map/ppermute | solution.py:373
  16.7 0.0 copy-start
  16.7 1.5 %collective-permute-done.l = f32[3,128,128]{2,1,0:T(8,128)S(1)} collective-permute-done((f32[3,128,128]{2,1,0:T(8,128)}, f32[3,128,128]{2,1,0:T(8,128)S(1)}, u32[]{:S(2)}, u32[]{:S(2)}) %collective-permute-start) | collective-permute-done | bytes 196640 | tf_op jit(solution)/shard_map/ppermute | solution.py:372
  18.2 0.0 copy-done
  18.2 0.0 copy-start.1
  18.2 0.7 copy-done.1
  18.9 7.6 %shard_map.131 = f32[2,176,128]{2,1,0:T(8,128)} custom-call(f32[8,128,128]{2,1,0:T(8,128)} %t.3, f32[8,128,128]{2,1,0:T(8,128)} %s.3, f32[8,128,128]{2,1,0:T(8,128)} %u.3, f32[8,128,128]{2,1,0:T(8,128)} %v.3, s32[8,128,128]{2,1,0:T(8,128)} %wet.3, f32[128,128]{1,0:T(8,128)} %mx.3, f32[128,128]{1,0:T(8,128)} %my.3, f32[3,128,128]{2,1,0:T(8,128)} %shard_map.129.c, ...), custom_call_target="tpu_custom_call" | custom-call | tf_op jit(solution)/shard_map/pallas_call | solution.py:378
  26.5 1.6 %fusion = (f32[1,176,128]{2,1,0:T(8,128)}, f32[176,128]{1,0:T(8,128)S(1)}, f32[176,128]{1,0:T(8,128)S(1)}) fusion(f32[2,176,128]{2,1,0:T(8,128)} %shard_map.131), kind=kLoop, calls=%fused_computation.3 | loop fusion | bytes 450560 | tf_op jit(solution)/shard_map/slice | solution.py:388
  28.1 0.0 all-gather.2.cloned.1.call-update
  28.1 0.0 copy-done.4
  28.3 3.1 %collective-permute-start.2 = (f32[176,128]{1,0:T(8,128)S(1)}, f32[176,128]{1,0:T(8,128)S(1)}, u32[]{:S(2)}, u32[]{:S(2)}) collective-permute-start(f32[176,128]{1,0:T(8,128)S(1)} %get-tuple-element.15), channel_id=1, source_target_pairs={{0,1},{2,3},{4,5},{6,7},{8,9},{10,11},{12,13},{14,15},{16,17},{18,... | collective-permute-start | bytes 270344 | tf_op jit(solution)/shard_map/ppermute | solution.py:388
  31.4 1.3 %collective-permute-start.3 = (f32[176,128]{1,0:T(8,128)S(1)}, f32[176,128]{1,0:T(8,128)S(1)}, u32[]{:S(2)}, u32[]{:S(2)}) collective-permute-start(f32[176,128]{1,0:T(8,128)S(1)} %get-tuple-element.16), channel_id=1, source_target_pairs={{1,0},{3,2},{5,4},{7,6},{9,8},{11,10},{13,12},{15,14},{17,16},{19,... | collective-permute-start | bytes 270344 | tf_op jit(solution)/shard_map/ppermute | solution.py:389
  32.7 0.6 pad_add_fusion.place
  33.4 27.2 %shard_map.130 = (f32[8,128,128]{2,1,0:T(8,128)}, f32[8,128,128]{2,1,0:T(8,128)}, f32[8,128,128]{2,1,0:T(8,128)}, f32[8,128,128]{2,1,0:T(8,128)}, f32[63,32,128]{2,1,0:T(8,128)}) custom-call(f32[4,8]{1,0:T(4,128)} %coef.3, f32[8,128,128]{2,1,0:T(8,128)} %t.3, f32[8,128,128]{2,1,0:T(8,128)} %s.3, f32[8,128,128]{2,1,0:T(8,128)} %u.3, f32[8,128,128]{2,1,0:T(8,128)} %v.3, ...), custom_call_target="tpu_custom_call" | custom-call | flops 60000000 | bytes 40000000 | tf_op jit(solution)/shard_map/pallas_call | solution.py:394
  60.6 0.0 collective-permute-done.2.from_south
  60.6 0.0 copy-start.2
  60.6 0.0 collective-permute-done.3.from_north
  60.6 0.0 copy-start.3
  60.6 9.9 %all-gather.2.cloned.1.call-done.fold = f32[16,176,128]{2,1,0:T(8,128)} async-done(((f32[1,176,128]{2,1,0:T(8,128)}), f32[16,176,128]{2,1,0:T(8,128)}) %all-gather.2.cloned.1.call-update) | async-done | bytes 1441808 | tf_op jit(solution)/shard_map/all_gather | solution.py:390
  70.5 0.0 copy-done.2
  70.5 0.0 copy-done.3
  70.5 4.0 %shard_map.132 = (f32[8,128,128]{2,1,0:T(8,128)}, f32[8,128,128]{2,1,0:T(8,128)}, f32[8,128,128]{2,1,0:T(8,128)}, f32[8,128,128]{2,1,0:T(8,128)}) custom-call(s32[2]{0:T(128)} %pad_add_fusion.place, f32[4,8]{1,0:T(4,128)} %coef.3, f32[7,128,128]{2,1,0:T(8,128)} %idf.3, ...), custom_call_target="tpu_custom_call", output_to_operand_aliasing={{0}: (7, {}), {1}: (8, {}), {2}: (9, {}), {3}: (10, {})} | custom-call | tf_op jit(solution)/shard_map/pallas_call | solution.py:417
Async XLA Ops:
  7.2 63.4 %all-gather.2.cloned.1.call-start = ((), (), s32[]{:S(2)}) async-start(), calls=%async_computation | async-start | bytes 1531904 | tf_op jit(solution)/shard_map/all_gather | solution.py:390
  10.5 17.6 %copy-start.4 = (s32[128]{0:T(128)S(1)}, s32[128]{0:T(128)}, u32[]{:S(2)}) copy-start(s32[128]{0:T(128)} %param.19) | copy-start | bytes 1540
  10.5 6.2 %collective-permute-start.1 = (f32[3,128,128]{2,1,0:T(8,128)}, f32[3,128,128]{2,1,0:T(8,128)S(1)}, u32[]{:S(2)}, u32[]{:S(2)}) collective-permute-start(f32[3,128,128]{2,1,0:T(8,128)} %shard_map.129.c), channel_id=1, source_target_pairs={{2,0},{4,2},{6,4},{8,6},{10,8},{12,10},{14,12},{16,14},{18,16},{20... | collective-permute-start | bytes 589832 | tf_op jit(solution)/shard_map/ppermute | solution.py:373
  10.6 7.6 %collective-permute-start = (f32[3,128,128]{2,1,0:T(8,128)}, f32[3,128,128]{2,1,0:T(8,128)S(1)}, u32[]{:S(2)}, u32[]{:S(2)}) collective-permute-start(f32[3,128,128]{2,1,0:T(8,128)} %shard_map.129.c), channel_id=1, source_target_pairs={{0,2},{2,4},{4,6},{6,8},{8,10},{10,12},{12,14},{14,16},{16,18},{18... | collective-permute-start | bytes 589832 | tf_op jit(solution)/shard_map/ppermute | solution.py:372
  16.7 1.5 %copy-start = (f32[3,128,128]{2,1,0:T(8,128)}, f32[3,128,128]{2,1,0:T(8,128)S(1)}, u32[]{:S(2)}) copy-start(f32[3,128,128]{2,1,0:T(8,128)S(1)} %collective-permute-done.1.r) | copy-start | bytes 589828
  18.2 0.7 copy-start.1
  28.3 32.3 %collective-permute-start.2 = (f32[176,128]{1,0:T(8,128)S(1)}, f32[176,128]{1,0:T(8,128)S(1)}, u32[]{:S(2)}, u32[]{:S(2)}) collective-permute-start(f32[176,128]{1,0:T(8,128)S(1)} %get-tuple-element.15), channel_id=1, source_target_pairs={{0,1},{2,3},{4,5},{6,7},{8,9},{10,11},{12,13},{14,15},{16,17},{18,... | collective-permute-start | bytes 270344 | tf_op jit(solution)/shard_map/ppermute | solution.py:388
  31.4 29.2 %collective-permute-start.3 = (f32[176,128]{1,0:T(8,128)S(1)}, f32[176,128]{1,0:T(8,128)S(1)}, u32[]{:S(2)}, u32[]{:S(2)}) collective-permute-start(f32[176,128]{1,0:T(8,128)S(1)} %get-tuple-element.16), channel_id=1, source_target_pairs={{1,0},{3,2},{5,4},{7,6},{9,8},{11,10},{13,12},{15,14},{17,16},{19,... | collective-permute-start | bytes 270344 | tf_op jit(solution)/shard_map/ppermute | solution.py:389
  60.6 10.0 %copy-start.2 = (f32[176,128]{1,0:T(8,128)}, f32[176,128]{1,0:T(8,128)S(1)}, u32[]{:S(2)}) copy-start(f32[176,128]{1,0:T(8,128)S(1)} %collective-permute-done.2.from_south) | copy-start | bytes 270340
  60.6 9.9 %copy-start.3 = (f32[176,128]{1,0:T(8,128)}, f32[176,128]{1,0:T(8,128)S(1)}, u32[]{:S(2)}) copy-start(f32[176,128]{1,0:T(8,128)S(1)} %collective-permute-done.3.from_north) | copy-start | bytes 270340
Sparse Core Ops, SparseCore 0:
  28.2 42.2 all-gather.1
